TPU v7x, 128 devices: a whole 4x4x4 slice. The times are simulated.
128 devices in a mesh: row: 8 (over z, x_hi), col: 16 (over x_lo, y, core).
Axes of the slice: x: 4 (x_hi: 2, x_lo: 2; x = x_hi * 2 + x_lo), y: 4, z: 4, core: 2. Of those that a mesh axis runs over, the one named last changes fastest.
Arguments:
- cycle_cells: int32 [2, 16384], P(None, ('row', 'col')), may hold values from 0 to 1023, as said below
- cycle_offsets: float32 [2, 16384], P(None, ('row', 'col')), may hold values from 0 to 1
- cycle_strength: float32 [16384], P(('row', 'col')), may hold values from -48 to 48
- block_tile: int32 [8192], P(('row', 'col')), may hold values from 0 to 127, as said below
Outputs:
- displacement: float32 [2, 16384], P(None, ('row', 'col'))
- diffused: float32 [4096, 8192], P('col', 'row')
- renewed: float32 [16384], P(('row', 'col'))
Inputs may be any that keep to these rules, and one draw needn't show every extreme that they name: Block b's cycles lie in the tile with slab block_tile[b] // 16 and radial part block_tile[b] mod 16. The blocks of one device name one tile at most 2 times and one slab at most 2 * 16 times; in every draw some slab is named 2 * 16 times by every device, each of its tiles twice. `cycle_cells`: row 0 is a radial cell within the cycle's tile, below 256; row 1 an axial cell, below 1024.
All inputs are finite; a program needn't handle non-finite values.
Results may differ from a plain program's by a relative error of at most 0.0004.
Values sent between devices are 32-bit elements; how exact they have to be, the bound alone decides.
A program may use at most 64 MiB of HBM per device.

v0:
```python
import math
import jax
import jax.numpy as jnp
from jax import lax
from jax.sharding import PartitionSpec as P

CR = 256
CZ = 1024
AGM_STEPS = 6
CORE_SQUARE = 4.0
STEP_LENGTH = 4.0
VISCOSITY = 0.2


def passed_along(block, axis, distance):
    devices = range(lax.axis_size(axis))
    route = [(i - distance, i) for i in devices if i - distance in devices]
    return lax.ppermute(block, axis, route)


def extended(shard, sides, width):
    for axis, dim in sides:
        peers, length = (lax.axis_size(axis), shard.shape[dim])
        up = [(i, (i + 1) % peers) for i in range(peers - 1)]
        down = [(j, i) for i, j in up]
        last = lax.slice_in_dim(shard, length - width, length, axis=dim)
        first = lax.slice_in_dim(shard, 0, width, axis=dim)
        before = lax.ppermute(last, axis, up)
        after = lax.ppermute(first, axis, down)
        shard = jnp.concatenate([before, shard, after], axis=dim)
    return shard


def tent_weight(distance):
    return jnp.maximum(1.0 - jnp.abs(distance), 0.0)


def pair_sums(targets, sources):
    target_r = targets[0][:, None]
    target_z = targets[1][:, None]
    source_r = sources[0][None, :]
    source_z = sources[1][None, :]
    source_gamma = sources[2][None, :]
    axial_gap = target_z - source_z
    smooth_sq = axial_gap * axial_gap + CORE_SQUARE
    radius_sum = target_r + source_r
    radius_gap = target_r - source_r
    far_sq = radius_sum * radius_sum + smooth_sq
    near_sq = radius_gap * radius_gap + smooth_sq
    modulus_sq = 4.0 * target_r * source_r / far_sq
    upper_mean = jnp.ones_like(far_sq)
    lower_mean = jnp.sqrt(near_sq / far_sq)
    series = 0.5 * modulus_sq
    factor = 1.0
    for agm_step in range(AGM_STEPS):
        half_gap = 0.5 * (upper_mean - lower_mean)
        upper_mean, lower_mean = (
            0.5 * (upper_mean + lower_mean),
            jnp.sqrt(upper_mean * lower_mean),
        )
        series = series + factor * half_gap * half_gap
        factor = factor * 2.0
    kind_first = 0.5 * math.pi / upper_mean
    kind_second = kind_first * (1.0 - series)
    prefactor = source_gamma / (2.0 * math.pi * jnp.sqrt(far_sq))
    square_sum = source_r * source_r + target_r * target_r + smooth_sq
    square_gap = source_r * source_r - target_r * target_r - smooth_sq
    axial_part = prefactor * (kind_first + square_gap / near_sq * kind_second)
    radial_part = (
        prefactor * axial_gap / target_r * (square_sum / near_sq * kind_second - kind_first)
    )
    return jnp.stack([jnp.sum(radial_part, axis=1), jnp.sum(axial_part, axis=1)])


def cycle_velocity(targets, sources):
    target_count = targets.shape[1]
    block_width = 512
    grouped = targets.reshape(2, target_count // block_width, block_width).transpose(1, 0, 2)
    result = lax.map(lambda target_group: pair_sums(target_group, sources), grouped)
    return result.transpose(1, 0, 2).reshape(2, target_count)


def diffuse(padded, first_row):
    center = padded[1:-1, 1:-1]
    outward = padded[2:, 1:-1]
    inward = padded[:-2, 1:-1]
    forward_z = padded[1:-1, 2:]
    backward_z = padded[1:-1, :-2]
    radius = jnp.maximum(first_row + jnp.arange(center.shape[0], dtype=jnp.int32), 1).astype(
        jnp.float32
    )[:, None]
    laplace = (
        outward
        + inward
        + forward_z
        + backward_z
        - 4.0 * center
        + (outward - inward) / (2.0 * radius)
        - center / (radius * radius)
    )
    return center + VISCOSITY * laplace


def rank_slots(group_of_block, capacity, per_block):
    block_count = group_of_block.shape[0]
    numbering = jnp.arange(block_count, dtype=jnp.int32)
    earlier = (group_of_block[:, None] == group_of_block[None, :]) & (
        numbering[None, :] < numbering[:, None]
    )
    standing = jnp.sum(earlier.astype(jnp.int32), axis=1)
    first_slot = (group_of_block * capacity + standing) * per_block
    return (first_slot[:, None] + jnp.arange(per_block, dtype=jnp.int32)[None, :]).reshape(-1)


def slot_matrix(cycle_slot, slot_total):
    return (jnp.arange(slot_total, dtype=jnp.int32)[None, :] == cycle_slot[:, None]).astype(
        jnp.float32
    )


def cycle_weights(cell, offset, anchor, total):
    grid_at = anchor + jnp.arange(total, dtype=jnp.int32)
    delta = (grid_at[:, None] - cell[None, :]).astype(jnp.float32)
    return tent_weight(offset[None, :] - delta)


def deposit_cycles(arrived, row_anchor, row_total, col_anchor, col_total):
    cycle_r = arrived[0].astype(jnp.int32)
    cycle_z = arrived[1].astype(jnp.int32)
    radial_weights = cycle_weights(cycle_r, arrived[2], row_anchor, row_total) * arrived[4][None, :]
    axial_weights = cycle_weights(cycle_z, arrived[3], col_anchor, col_total)
    return lax.dot_general(
        radial_weights,
        axial_weights,
        (((1,), (1,)), ((), ())),
        precision=lax.Precision.HIGHEST,
        preferred_element_type=jnp.float32,
    )


def sample_field(field_part, arrived, row_anchor, col_anchor):
    cycle_r = arrived[0].astype(jnp.int32)
    cycle_z = arrived[1].astype(jnp.int32)
    radial_weights = cycle_weights(cycle_r, arrived[2], row_anchor, field_part.shape[0])
    axial_weights = cycle_weights(cycle_z, arrived[3], col_anchor, field_part.shape[1])
    along_rows = jnp.dot(
        field_part,
        axial_weights,
        precision=lax.Precision.HIGHEST,
        preferred_element_type=jnp.float32,
    )
    return jnp.sum(radial_weights * along_rows, axis=0)


def on_device(cycle_cells, cycle_offsets, cycle_strength, block_tile):
    row_devices = lax.axis_size("row")
    col_devices = lax.axis_size("col")
    per_block = cycle_cells.shape[1] // block_tile.shape[0]
    cycle_tile = jnp.repeat(block_tile, per_block)
    cell_r = jnp.clip(cycle_tile % col_devices * CR + cycle_cells[0], 16, CR * col_devices - 3)
    cell_z = jnp.clip(cycle_tile // col_devices * CZ + cycle_cells[1], 2, CZ * row_devices - 3)
    positions = jnp.stack(
        [
            cell_r.astype(jnp.float32) + cycle_offsets[0],
            cell_z.astype(jnp.float32) + cycle_offsets[1],
        ]
    )
    own_sources = jnp.concatenate([positions, cycle_strength[None, :]], axis=0)
    row_targets = lax.all_gather(positions, "col", axis=1, tiled=True)
    partial_sums = cycle_velocity(
        row_targets, lax.all_gather(own_sources, "row", axis=1, tiled=True)
    )
    velocity = lax.psum_scatter(partial_sums, "col", scatter_dimension=1, tiled=True)
    displacement = STEP_LENGTH * velocity
    moved_offsets = jnp.clip(cycle_offsets + displacement, -1.0, 2.0)
    payload = jnp.stack(
        [
            cell_r.astype(jnp.float32),
            cell_z.astype(jnp.float32),
            moved_offsets[0],
            moved_offsets[1],
            cycle_strength,
        ]
    )
    row_start = lax.axis_index("col") * CR
    col_start = lax.axis_index("row") * CZ
    cycle_slot = rank_slots(block_tile // col_devices, 2 * col_devices, per_block)
    slot_table = slot_matrix(cycle_slot, row_devices * 2 * col_devices * per_block)
    outgoing = jnp.dot(
        payload, slot_table, precision=lax.Precision.HIGHEST, preferred_element_type=jnp.float32
    )
    arrived = lax.all_to_all(outgoing, "row", split_axis=1, concat_axis=1, tiled=True)
    folded_r = lax.psum_scatter(
        deposit_cycles(arrived, jnp.int32(0), CR * lax.axis_size("col"), col_start - 1, CZ + 3),
        "col",
        scatter_dimension=0,
        tiled=True,
    )
    from_next_z = passed_along(folded_r[:, 0:1], "row", -1)
    from_prev_z = passed_along(folded_r[:, CZ + 1 : CZ + 3], "row", 1)
    deposited = folded_r[:, 1 : CZ + 1]
    deposited = deposited.at[:, CZ - 1 : CZ].add(from_next_z)
    deposited = deposited.at[:, 0:2].add(from_prev_z)
    padded = extended(deposited, (("row", 1), ("col", 0)), 1)
    diffused = diffuse(padded, row_start)
    widened = extended(diffused, (("row", 1),), 2)
    values = sample_field(
        lax.all_gather(widened, "col", axis=0, tiled=True), arrived, jnp.int32(0), col_start - 2
    )
    returned = lax.all_to_all(values, "row", split_axis=0, concat_axis=0, tiled=True)
    renewed = jnp.dot(
        slot_table, returned, precision=lax.Precision.HIGHEST, preferred_element_type=jnp.float32
    )
    return (displacement, diffused, renewed)


def solution(mesh):
    in_specs = (
        P(None, ("row", "col")),
        P(None, ("row", "col")),
        P(("row", "col")),
        P(("row", "col")),
    )
    out_specs = (P(None, ("row", "col")), P("col", "row"), P(("row", "col")))
    return jax.shard_map(
        on_device, mesh=mesh, in_specs=in_specs, out_specs=out_specs, check_vma=False
    )
```

profile of v0, /device:TPU:0, one launch (start us, length us, event | category | flops | bytes accessed | tf_op | source)
XLA Modules:
  0.0 520.6 jit_solution(1767718619613536940)
XLA Ops:
  7.2 0.7 broadcast_in_dim.20
  8.1 0.8 slice_add_fusion.2
  8.9 0.7 pad_maximum_fusion.4
  9.6 32.1 %all_gather.9 = f32[3,1024]{1,0:T(4,128)S(1)} all-gather(f32[3,128]{1,0:T(4,128)S(1)} %pad_maximum_fusion.4), channel_id=1, replica_groups=mesh['row'=8,'col'=16] {'row'}, dimensions={1}, use_global_device_ids=true | all-gather | bytes 13824 | tf_op jit(solution)/shard_map/all_gather | solution.py:171
  41.6 19.8 %all_gather.10 = f32[2,2048]{1,0:T(2,128)S(1)} all-gather(f32[2,128]{1,0:T(2,128)S(1)} %pad_maximum_fusion.5), channel_id=1, replica_groups=mesh['row'=8,'col'=16] {'col'}, dimensions={1}, use_global_device_ids=true | all-gather | bytes 17408 | tf_op jit(solution)/shard_map/all_gather | solution.py:169
  61.5 39.3 %while.14 = (s32[]{:T(128)}, f32[4,2,512]{2,1,0:T(2,128)S(1)}, f32[3,1024]{1,0:T(4,128)S(1)}, f32[4,2,512]{2,1,0:T(2,128)S(1)}, f32[1,1024]{1,0:T(1,128)S(1)}, /*index=5*/s32[]{:T(128)}, s32[]{:T(128)}, s32[]{}) while((s32[]{:T(128)}, f32[4,2,512]{2,1,0:T(2,128)S(1)}, f32[3,1024]{1,0:T(4,128)S(1)}, f32[4,2,512]{2,1,0:T(2,128)S(1)}, ...), condition=%wide.region_3.4_spmd, body=%wide.region_0.3_spmd.sunk | while | flops 40895488 | bytes 75893 | solution.py:79
  61.5 9.7 %fusion.90 = (f32[512]{0:T(512)S(1)}, f32[512]{0:T(512)S(1)}) fusion(f32[512]{0:T(512)S(1)} %get-tuple-element.184, f32[1024]{0:T(1024)S(1)} %bitcast.64, f32[1024]{0:T(1024)S(1)} %bitcast.54, f32[512]{0:T(512)S(1)} %bitcast.62, f32[1024]{0:T(1024)S(1)} %bitcast.55, f32[512]{0:T(512)S(1)} %bitcast.51, f32[512]{0:T(512)S(1)} %get-tuple-element.188, ...), kind=kLoop, calls=%fused_computation.38.clone.1 | loop fusion | flops 40893440 | bytes 28672 | tf_op jit(solution)/shard_map/while/body/eval_jaxpr/reduce_sum | solution.py:72
  71.3 9.7 %fusion.90 = (f32[512]{0:T(512)S(1)}, f32[512]{0:T(512)S(1)}) fusion(f32[512]{0:T(512)S(1)} %get-tuple-element.184, f32[1024]{0:T(1024)S(1)} %bitcast.64, f32[1024]{0:T(1024)S(1)} %bitcast.54, f32[512]{0:T(512)S(1)} %bitcast.62, f32[1024]{0:T(1024)S(1)} %bitcast.55, f32[512]{0:T(512)S(1)} %bitcast.51, f32[512]{0:T(512)S(1)} %get-tuple-element.188, ...), kind=kLoop, calls=%fused_computation.38.clone.1 | loop fusion | flops 40893440 | bytes 28672 | tf_op jit(solution)/shard_map/while/body/eval_jaxpr/reduce_sum | solution.py:72
  81.2 9.7 %fusion.90 = (f32[512]{0:T(512)S(1)}, f32[512]{0:T(512)S(1)}) fusion(f32[512]{0:T(512)S(1)} %get-tuple-element.184, f32[1024]{0:T(1024)S(1)} %bitcast.64, f32[1024]{0:T(1024)S(1)} %bitcast.54, f32[512]{0:T(512)S(1)} %bitcast.62, f32[1024]{0:T(1024)S(1)} %bitcast.55, f32[512]{0:T(512)S(1)} %bitcast.51, f32[512]{0:T(512)S(1)} %get-tuple-element.188, ...), kind=kLoop, calls=%fused_computation.38.clone.1 | loop fusion | flops 40893440 | bytes 28672 | tf_op jit(solution)/shard_map/while/body/eval_jaxpr/reduce_sum | solution.py:72
  91.0 9.8 %fusion.90 = (f32[512]{0:T(512)S(1)}, f32[512]{0:T(512)S(1)}) fusion(f32[512]{0:T(512)S(1)} %get-tuple-element.184, f32[1024]{0:T(1024)S(1)} %bitcast.64, f32[1024]{0:T(1024)S(1)} %bitcast.54, f32[512]{0:T(512)S(1)} %bitcast.62, f32[1024]{0:T(1024)S(1)} %bitcast.55, f32[512]{0:T(512)S(1)} %bitcast.51, f32[512]{0:T(512)S(1)} %get-tuple-element.188, ...), kind=kLoop, calls=%fused_computation.38.clone.1 | loop fusion | flops 40893440 | bytes 28672 | tf_op jit(solution)/shard_map/while/body/eval_jaxpr/reduce_sum | solution.py:72
  100.8 1.3 copy.31
  102.7 57.9 %reduce-scatter.7.cloned.1.call-done = f32[128,2]{1,0:T(8,128)} async-done(((f32[2048,2]{1,0:T(8,128)}), f32[128,2]{1,0:T(8,128)}) %reduce-scatter.7.cloned.1.call-update) | async-done | bytes 1040
  160.6 0.9 copy.32
  162.4 0.7 reshape.303
  163.1 6.6 %all-to-all-start = ((f32[8,1,320]{2,1,0:T(1,128)}), f32[8,1,320]{2,1,0:T(1,128)S(1)}, u32[]{:S(2)}, u32[]{:S(2)}) async-start(f32[8,1,320]{2,1,0:T(1,128)} %reshape.303), calls=%async_computation | async-start | bytes 24576 | tf_op jit(solution)/shard_map/all_to_all | solution.py:192
  169.9 7.5 %all-to-all-done = f32[8,1,320]{2,1,0:T(1,128)S(1)} async-done(((f32[8,1,320]{2,1,0:T(1,128)}), f32[8,1,320]{2,1,0:T(1,128)S(1)}, u32[]{:S(2)}, u32[]{:S(2)}) %all-to-all-start) | async-done | bytes 10272 | tf_op jit(solution)/shard_map/all_to_all | solution.py:192
  177.9 0.7 reduce.34
  179.1 37.6 %fusion.25 = f32[4096,1027]{0,1:T(8,128)} fusion(f32[512]{0:T(512)S(1)} %mul.386, s32[512]{0:T(512)S(1)} %convert_element_type.62, f32[512]{0:T(512)S(1)} %sub.233, s32[512]{0:T(512)S(1)} %convert_element_type.65, s32[1027]{0:T(1024)S(1)} %iota_add_fusion.2, f32[512]{0:T(512)S(1)} %sub.241), kind=kOutput, calls=%fused_computation.45 | convolution fusion | flops 25863135232 | bytes 16840716 | tf_op jit(solution)/shard_map/dot_general | solution.py:132
  216.7 93.5 %reduce-scatter.5.cloned.1.call-done = f32[256,1027]{0,1:T(8,128)} async-done(((f32[4096,1027]{0,1:T(8,128)}), f32[256,1027]{0,1:T(8,128)}) %reduce-scatter.5.cloned.1.call-update) | async-done | bytes 1051664 | tf_op jit(solution)/shard_map/reduce_scatter | solution.py:193
  310.2 0.7 slice.190
  310.9 1.3 collective-permute-start
  312.9 0.7 slice.192
  313.6 6.0 %collective-permute-start.1 = (f32[256,2]{0,1:T(2,128)S(1)}, f32[256,2]{0,1:T(2,128)S(1)}, u32[]{:S(2)}, u32[]{:S(2)}) collective-permute-start(f32[256,2]{0,1:T(2,128)S(1)} %slice.192), channel_id=1, source_target_pairs={{0,16},{16,32},{32,48},{48,64},{64,80},{80,96},{96,112},{1,17},{17... | collective-permute-start | bytes 6152 | tf_op jit(solution)/shard_map/ppermute | solution.py:18
  319.6 1.3 slice.188
  320.9 0.7 slice_add_fusion
  322.3 5.5 %collective-permute-start.2 = (f32[256,1]{0,1:T(1,128)S(1)}, f32[256,1]{0,1:T(1,128)S(1)}, u32[]{:S(2)}, u32[]{:S(2)}) collective-permute-start(f32[256,1]{0,1:T(1,128)S(1)} %slice.193), channel_id=1, source_target_pairs={{0,16},{16,32},{32,48},{48,64},{64,80},{80,96},{96,112},{1,17},{17... | collective-permute-start | bytes 3080 | tf_op jit(solution)/shard_map/ppermute | solution.py:28
  327.8 1.3 collective-permute-start.3
  329.2 6.1 %collective-permute-done.3 = f32[256,1]{0,1:T(1,128)S(1)} collective-permute-done((f32[256,1]{0,1:T(1,128)S(1)}, f32[256,1]{0,1:T(1,128)S(1)}, u32[]{:S(2)}, u32[]{:S(2)}) %collective-permute-start.3) | collective-permute-done | bytes 1056 | tf_op jit(solution)/shard_map/ppermute | solution.py:29
  335.2 0.9 concatenate.28
  336.1 0.9 fusion.82
  337.1 1.2 copy.25
  338.3 1.3 collective-permute-start.4
  339.8 3.0 collective-permute-start.5
  342.9 1.0 copy.26
  343.9 1.0 copy.28
  345.0 2.2 fusion.59
  347.2 6.3 %collective-permute-start.6 = (f32[256,2]{0,1:T(2,128)S(1)}, f32[256,2]{0,1:T(2,128)S(1)}, u32[]{:S(2)}, u32[]{:S(2)}) collective-permute-start(f32[256,2]{0,1:T(2,128)S(1)} %get-tuple-element.138), channel_id=1, source_target_pairs={{0,16},{16,32},{32,48},{48,64},{64,80},{80,96},{96,112},{1,17},{17... | collective-permute-start | bytes 6152 | tf_op jit(solution)/shard_map/ppermute | solution.py:28
  353.5 1.3 collective-permute-start.7
  354.8 5.7 %collective-permute-done.7 = f32[256,2]{0,1:T(2,128)S(1)} collective-permute-done((f32[256,2]{0,1:T(2,128)S(1)}, f32[256,2]{0,1:T(2,128)S(1)}, u32[]{:S(2)}, u32[]{:S(2)}) %collective-permute-start.7) | collective-permute-done | bytes 2080 | tf_op jit(solution)/shard_map/ppermute | solution.py:29
  360.5 4.9 concatenate.33
  365.4 92.0 %all-gather.2.cloned.1.call-done = f32[4096,1028]{0,1:T(8,128)} async-done(((f32[256,1028]{0,1:T(8,128)}), f32[4096,1028]{0,1:T(8,128)}) %all-gather.2.cloned.1.call-update) | async-done | bytes 16842768 | tf_op jit(solution)/shard_map/all_gather | solution.py:208
  457.4 39.4 %multiply_reduce_fusion = f32[512]{0:T(512)S(1)} fusion(f32[4096,1028]{0,1:T(8,128)} %all-gather.2.cloned.1.call-done, s32[512]{0:T(512)S(1)} %convert_element_type.62, f32[512]{0:T(512)S(1)} %sub.233, s32[512]{0:T(512)S(1)} %convert_element_type.65, s32[1028]{0:T(1024)S(1)} %iota_add_fusion.1, f32[512]{0:T(512)S(1)} %sub.241), kind=kOutput, calls=%fused_computation.44 | convolution fusion | flops 25890402304 | bytes 16857104 | tf_op jit(solution)/shard_map/dot_general | solution.py:146
  496.9 0.7 all_to_all.16
  497.5 6.8 %all-to-all-start.1 = ((f32[8,64,1]{1,2,0:T(1,128)}), f32[8,64,1]{1,2,0:T(1,128)S(1)}, u32[]{:S(2)}, u32[]{:S(2)}) async-start(f32[8,64,1]{1,2,0:T(1,128)} %bitcast.14), calls=%async_computation.2 | async-start | bytes 8192 | tf_op jit(solution)/shard_map/all_to_all | solution.py:210
  504.4 1.3 copy.30
  505.7 6.4 %all-to-all-done.1 = f32[8,64,1]{1,2,0:T(1,128)S(1)} async-done(((f32[8,64,1]{1,2,0:T(1,128)}), f32[8,64,1]{1,2,0:T(1,128)S(1)}, u32[]{:S(2)}, u32[]{:S(2)}) %all-to-all-start.1) | async-done | bytes 2080 | tf_op jit(solution)/shard_map/all_to_all | solution.py:210
  512.5 0.7 reduce.33
  513.3 0.8 convolution_bitcast_fusion
  (68 shorter events, 5.2 us)
Async XLA Ops:
  7.2 153.4 %reduce-scatter.7.cloned.1.call-start = ((), (), s32[]{:S(2)}) async-start(), calls=%async_computation.6 | async-start | bytes 1114112
  100.8 1.4 copy-start.1
  100.8 60.6 %copy-start = (f32[2,128]{1,0:T(2,128)S(1)}, f32[2,128]{1,0:T(2,128)}, u32[]{:S(2)}) copy-start(f32[2,128]{1,0:T(2,128)} %param.11) | copy-start | bytes 3076
  100.8 61.2 %copy-start.2 = (f32[128]{0:T(128)S(1)}, f32[128]{0:T(128)}, u32[]{:S(2)}) copy-start(f32[128]{0:T(128)} %param.12) | copy-start | bytes 1540
  163.1 14.3 %all-to-all-start = ((f32[8,1,320]{2,1,0:T(1,128)}), f32[8,1,320]{2,1,0:T(1,128)S(1)}, u32[]{:S(2)}, u32[]{:S(2)}) async-start(f32[8,1,320]{2,1,0:T(1,128)} %reshape.303), calls=%async_computation | async-start | bytes 24576 | tf_op jit(solution)/shard_map/all_to_all | solution.py:192
  169.6 140.6 %reduce-scatter.5.cloned.1.call-start = ((), (), s32[]{:S(2)}) async-start(), calls=%async_computation.4 | async-start | bytes 17965056 | tf_op jit(solution)/shard_map/reduce_scatter | solution.py:193
  216.7 240.7 %all-gather.2.cloned.1.call-start = ((), (), s32[]{:S(2)}) async-start(), calls=%async_computation.5 | async-start | bytes 17965056 | tf_op jit(solution)/shard_map/all_gather | solution.py:208
  310.9 10.0 %collective-permute-start = (f32[256,1]{0,1:T(1,128)S(1)}, f32[256,1]{0,1:T(1,128)S(1)}, u32[]{:S(2)}, u32[]{:S(2)}) collective-permute-start(f32[256,1]{0,1:T(1,128)S(1)} %slice.190), channel_id=1, source_target_pairs={{16,0},{32,16},{48,32},{64,48},{80,64},{96,80},{112,96},{17,1},{33... | collective-permute-start | bytes 3080 | tf_op jit(solution)/shard_map/ppermute | solution.py:18
  313.6 8.1 %collective-permute-start.1 = (f32[256,2]{0,1:T(2,128)S(1)}, f32[256,2]{0,1:T(2,128)S(1)}, u32[]{:S(2)}, u32[]{:S(2)}) collective-permute-start(f32[256,2]{0,1:T(2,128)S(1)} %slice.192), channel_id=1, source_target_pairs={{0,16},{16,32},{32,48},{48,64},{64,80},{80,96},{96,112},{1,17},{17... | collective-permute-start | bytes 6152 | tf_op jit(solution)/shard_map/ppermute | solution.py:18
  322.3 6.8 %collective-permute-start.2 = (f32[256,1]{0,1:T(1,128)S(1)}, f32[256,1]{0,1:T(1,128)S(1)}, u32[]{:S(2)}, u32[]{:S(2)}) collective-permute-start(f32[256,1]{0,1:T(1,128)S(1)} %slice.193), channel_id=1, source_target_pairs={{0,16},{16,32},{32,48},{48,64},{64,80},{80,96},{96,112},{1,17},{17... | collective-permute-start | bytes 3080 | tf_op jit(solution)/shard_map/ppermute | solution.py:28
  327.8 7.4 %collective-permute-start.3 = (f32[256,1]{0,1:T(1,128)S(1)}, f32[256,1]{0,1:T(1,128)S(1)}, u32[]{:S(2)}, u32[]{:S(2)}) collective-permute-start(f32[256,1]{0,1:T(1,128)S(1)} %slice.194), channel_id=1, source_target_pairs={{16,0},{32,16},{48,32},{64,48},{80,64},{96,80},{112,96},{17,1},{33... | collective-permute-start | bytes 3080 | tf_op jit(solution)/shard_map/ppermute | solution.py:29
  338.3 4.6 collective-permute-start.4
  339.8 4.1 collective-permute-start.5
  347.2 7.6 %collective-permute-start.6 = (f32[256,2]{0,1:T(2,128)S(1)}, f32[256,2]{0,1:T(2,128)S(1)}, u32[]{:S(2)}, u32[]{:S(2)}) collective-permute-start(f32[256,2]{0,1:T(2,128)S(1)} %get-tuple-element.138), channel_id=1, source_target_pairs={{0,16},{16,32},{32,48},{48,64},{64,80},{80,96},{96,112},{1,17},{17... | collective-permute-start | bytes 6152 | tf_op jit(solution)/shard_map/ppermute | solution.py:28
  353.5 7.0 %collective-permute-start.7 = (f32[256,2]{0,1:T(2,128)S(1)}, f32[256,2]{0,1:T(2,128)S(1)}, u32[]{:S(2)}, u32[]{:S(2)}) collective-permute-start(f32[256,2]{0,1:T(2,128)S(1)} %get-tuple-element.137), channel_id=1, source_target_pairs={{16,0},{32,16},{48,32},{64,48},{80,64},{96,80},{112,96},{17,1},{33... | collective-permute-start | bytes 6152 | tf_op jit(solution)/shard_map/ppermute | solution.py:29
  497.5 14.5 %all-to-all-start.1 = ((f32[8,64,1]{1,2,0:T(1,128)}), f32[8,64,1]{1,2,0:T(1,128)S(1)}, u32[]{:S(2)}, u32[]{:S(2)}) async-start(f32[8,64,1]{1,2,0:T(1,128)} %bitcast.14), calls=%async_computation.2 | async-start | bytes 8192 | tf_op jit(solution)/shard_map/all_to_all | solution.py:210
Sparse Core Ops, SparseCore 0:
  102.3 58.1 reduce-scatter.6
  216.8 93.3 reduce-scatter.4
  365.5 91.8 all-gather.1
where the time goes:
time: 522 us; the launch traced here: 521 us
  waiting for transfers between devices  269 us (52%)
  matrix products  78.1 us (15%)
  blocking collectives  51.9 us (10%)
  other arithmetic  47 us (9%)
  starting transfers between devices  39.8 us (8%)
  local copies, waits for them, and re-layouts  20.7 us (4%)
  between operations  14 us (3%)
    reduce_scatter x1, waiting for transfers between devices, on_device(): lax.psum_scatter(deposit_cycles(arrived, jnp.int32(0), CR * lax.axis_size...  93.5 us
    all_gather x1, waiting for transfers between devices, on_device(): lax.all_gather(widened, 'col', axis=0, tiled=True)  92 us
    unnamed x4, waiting for transfers between devices  57.9 us
    dot_general x1, matrix products, sample_field(): jnp.dot(field_part, axial_weights, precision=lax.Precision.HIGHEST, prefe...  39.4 us
    reduce_sum x4, other arithmetic, pair_sums(): jnp.sum(radial_part, axis=1)  39 us
    dot_general x1, matrix products, deposit_cycles(): lax.dot_general(radial_weights, axial_weights, (((1,), (1,)), ((), ())),...  37.6 us
    all_gather x1, blocking collectives, on_device(): lax.all_gather(own_sources, 'row', axis=1, tiled=True)  32.1 us
    all_gather x1, blocking collectives, on_device(): row_targets = lax.all_gather(positions, 'col', axis=1, tiled=True)  19.8 us
  transfers between devices with their start and end apart: 13, of which 7 were waited for; matrix products, arithmetic and copies ran while one was open for 1% of the time, Pallas kernels for 0%

commit v1 on v0

--- a/solution.py
+++ b/solution.py
@@ -189,7 +189,10 @@
     outgoing = jnp.dot(
         payload, slot_table, precision=lax.Precision.HIGHEST, preferred_element_type=jnp.float32
     )
-    arrived = lax.all_to_all(outgoing, "row", split_axis=1, concat_axis=1, tiled=True)
+    arrived = jnp.concatenate(
+        lax.all_to_all(jnp.stack(jnp.split(outgoing, lax.axis_size("row"), axis=1)), "row", 0, 0),
+        axis=1,
+    )
     folded_r = lax.psum_scatter(
         deposit_cycles(arrived, jnp.int32(0), CR * lax.axis_size("col"), col_start - 1, CZ + 3),
         "col",

time: 522 us -> 522 us (level)
  no operation moved by 1% of the time
where the time goes in v1:
time: 522 us; the launch traced here: 521 us
  waiting for transfers between devices  269 us (52%)
  matrix products  78.1 us (15%)
  blocking collectives  51.9 us (10%)
  other arithmetic  47 us (9%)
  starting transfers between devices  39.7 us (8%)
  local copies, waits for them, and re-layouts  20.9 us (4%)
  between operations  14 us (3%)
    reduce_scatter x1, waiting for transfers between devices, on_device(): lax.psum_scatter(deposit_cycles(arrived, jnp.int32(0), CR * lax.axis_size...  93.5 us
    all_gather x1, waiting for transfers between devices, on_device(): lax.all_gather(widened, 'col', axis=0, tiled=True)  92 us
    unnamed x4, waiting for transfers between devices  57.9 us
    dot_general x1, matrix products, sample_field(): jnp.dot(field_part, axial_weights, precision=lax.Precision.HIGHEST, prefe...  39.5 us
    reduce_sum x4, other arithmetic, pair_sums(): jnp.sum(radial_part, axis=1)  39 us
    dot_general x1, matrix products, deposit_cycles(): lax.dot_general(radial_weights, axial_weights, (((1,), (1,)), ((), ())),...  37.6 us
    all_gather x1, blocking collectives, on_device(): lax.all_gather(own_sources, 'row', axis=1, tiled=True)  32.1 us
    all_gather x1, blocking collectives, on_device(): row_targets = lax.all_gather(positions, 'col', axis=1, tiled=True)  19.8 us
  transfers between devices with their start and end apart: 13, of which 7 were waited for; matrix products, arithmetic and copies ran while one was open for 1% of the time, Pallas kernels for 0%

profile of v1, /device:TPU:0, one launch (start us, length us, event | category | flops | bytes accessed | tf_op | source)
XLA Modules:
  0.0 520.9 jit_solution(18301740788495701397)
XLA Ops:
  7.2 0.7 broadcast_in_dim.20
  8.1 0.8 slice_add_fusion.2
  8.9 0.7 pad_maximum_fusion.4
  9.6 32.1 %all_gather.9 = f32[3,1024]{1,0:T(4,128)S(1)} all-gather(f32[3,128]{1,0:T(4,128)S(1)} %pad_maximum_fusion.4), channel_id=1, replica_groups=mesh['row'=8,'col'=16] {'row'}, dimensions={1}, use_global_device_ids=true | all-gather | bytes 13824 | tf_op jit(solution)/shard_map/all_gather | solution.py:171
  41.6 19.8 %all_gather.10 = f32[2,2048]{1,0:T(2,128)S(1)} all-gather(f32[2,128]{1,0:T(2,128)S(1)} %pad_maximum_fusion.5), channel_id=1, replica_groups=mesh['row'=8,'col'=16] {'col'}, dimensions={1}, use_global_device_ids=true | all-gather | bytes 17408 | tf_op jit(solution)/shard_map/all_gather | solution.py:169
  61.5 39.3 %while.14 = (s32[]{:T(128)}, f32[4,2,512]{2,1,0:T(2,128)S(1)}, f32[3,1024]{1,0:T(4,128)S(1)}, f32[4,2,512]{2,1,0:T(2,128)S(1)}, f32[1,1024]{1,0:T(1,128)S(1)}, /*index=5*/s32[]{:T(128)}, s32[]{:T(128)}, s32[]{}) while((s32[]{:T(128)}, f32[4,2,512]{2,1,0:T(2,128)S(1)}, f32[3,1024]{1,0:T(4,128)S(1)}, f32[4,2,512]{2,1,0:T(2,128)S(1)}, ...), condition=%wide.region_3.4_spmd, body=%wide.region_0.3_spmd.sunk | while | flops 40895488 | bytes 75893 | solution.py:79
  61.5 9.7 %fusion.90 = (f32[512]{0:T(512)S(1)}, f32[512]{0:T(512)S(1)}) fusion(f32[512]{0:T(512)S(1)} %get-tuple-element.184, f32[1024]{0:T(1024)S(1)} %bitcast.92, f32[1024]{0:T(1024)S(1)} %bitcast.82, f32[512]{0:T(512)S(1)} %bitcast.90, f32[1024]{0:T(1024)S(1)} %bitcast.83, f32[512]{0:T(512)S(1)} %bitcast.80, f32[512]{0:T(512)S(1)} %get-tuple-element.188, ...), kind=kLoop, calls=%fused_computation.38.clone.1 | loop fusion | flops 40893440 | bytes 28672 | tf_op jit(solution)/shard_map/while/body/eval_jaxpr/reduce_sum | solution.py:72
  71.3 9.7 %fusion.90 = (f32[512]{0:T(512)S(1)}, f32[512]{0:T(512)S(1)}) fusion(f32[512]{0:T(512)S(1)} %get-tuple-element.184, f32[1024]{0:T(1024)S(1)} %bitcast.92, f32[1024]{0:T(1024)S(1)} %bitcast.82, f32[512]{0:T(512)S(1)} %bitcast.90, f32[1024]{0:T(1024)S(1)} %bitcast.83, f32[512]{0:T(512)S(1)} %bitcast.80, f32[512]{0:T(512)S(1)} %get-tuple-element.188, ...), kind=kLoop, calls=%fused_computation.38.clone.1 | loop fusion | flops 40893440 | bytes 28672 | tf_op jit(solution)/shard_map/while/body/eval_jaxpr/reduce_sum | solution.py:72
  81.2 9.7 %fusion.90 = (f32[512]{0:T(512)S(1)}, f32[512]{0:T(512)S(1)}) fusion(f32[512]{0:T(512)S(1)} %get-tuple-element.184, f32[1024]{0:T(1024)S(1)} %bitcast.92, f32[1024]{0:T(1024)S(1)} %bitcast.82, f32[512]{0:T(512)S(1)} %bitcast.90, f32[1024]{0:T(1024)S(1)} %bitcast.83, f32[512]{0:T(512)S(1)} %bitcast.80, f32[512]{0:T(512)S(1)} %get-tuple-element.188, ...), kind=kLoop, calls=%fused_computation.38.clone.1 | loop fusion | flops 40893440 | bytes 28672 | tf_op jit(solution)/shard_map/while/body/eval_jaxpr/reduce_sum | solution.py:72
  91.0 9.8 %fusion.90 = (f32[512]{0:T(512)S(1)}, f32[512]{0:T(512)S(1)}) fusion(f32[512]{0:T(512)S(1)} %get-tuple-element.184, f32[1024]{0:T(1024)S(1)} %bitcast.92, f32[1024]{0:T(1024)S(1)} %bitcast.82, f32[512]{0:T(512)S(1)} %bitcast.90, f32[1024]{0:T(1024)S(1)} %bitcast.83, f32[512]{0:T(512)S(1)} %bitcast.80, f32[512]{0:T(512)S(1)} %get-tuple-element.188, ...), kind=kLoop, calls=%fused_computation.38.clone.1 | loop fusion | flops 40893440 | bytes 28672 | tf_op jit(solution)/shard_map/while/body/eval_jaxpr/reduce_sum | solution.py:72
  100.8 1.3 copy.29
  102.7 57.9 %reduce-scatter.7.cloned.1.call-done = f32[128,2]{1,0:T(8,128)} async-done(((f32[2048,2]{1,0:T(8,128)}), f32[128,2]{1,0:T(8,128)}) %reduce-scatter.7.cloned.1.call-update) | async-done | bytes 1040
  160.6 0.9 copy.30
  162.6 0.7 reshape.310
  163.3 6.6 %all-to-all-start = ((f32[8,1,320]{2,1,0:T(1,128)}), f32[8,1,320]{2,1,0:T(1,128)S(1)}, u32[]{:S(2)}, u32[]{:S(2)}) async-start(f32[8,1,320]{2,1,0:T(1,128)} %reshape.310), calls=%async_computation | async-start | bytes 24576 | tf_op jit(solution)/shard_map/all_to_all | solution.py:193
  170.1 7.5 %all-to-all-done = f32[8,1,320]{2,1,0:T(1,128)S(1)} async-done(((f32[8,1,320]{2,1,0:T(1,128)}), f32[8,1,320]{2,1,0:T(1,128)S(1)}, u32[]{:S(2)}, u32[]{:S(2)}) %all-to-all-start) | async-done | bytes 10272 | tf_op jit(solution)/shard_map/all_to_all | solution.py:193
  178.1 0.7 reduce.34
  179.3 37.6 %fusion.25 = f32[4096,1027]{0,1:T(8,128)} fusion(f32[512]{0:T(512)S(1)} %mul.386, s32[512]{0:T(512)S(1)} %convert_element_type.62, f32[512]{0:T(512)S(1)} %sub.233, s32[512]{0:T(512)S(1)} %convert_element_type.65, s32[1027]{0:T(1024)S(1)} %iota_add_fusion.2, f32[512]{0:T(512)S(1)} %sub.241), kind=kOutput, calls=%fused_computation.45 | convolution fusion | flops 25863135232 | bytes 16840716 | tf_op jit(solution)/shard_map/dot_general | solution.py:132
  216.9 93.5 %reduce-scatter.5.cloned.1.call-done = f32[256,1027]{0,1:T(8,128)} async-done(((f32[4096,1027]{0,1:T(8,128)}), f32[256,1027]{0,1:T(8,128)}) %reduce-scatter.5.cloned.1.call-update) | async-done | bytes 1051664 | tf_op jit(solution)/shard_map/reduce_scatter | solution.py:196
  310.5 0.7 slice.190
  311.2 1.3 collective-permute-start
  313.1 0.7 slice.192
  313.8 6.0 %collective-permute-start.1 = (f32[256,2]{0,1:T(2,128)S(1)}, f32[256,2]{0,1:T(2,128)S(1)}, u32[]{:S(2)}, u32[]{:S(2)}) collective-permute-start(f32[256,2]{0,1:T(2,128)S(1)} %slice.192), channel_id=1, source_target_pairs={{0,16},{16,32},{32,48},{48,64},{64,80},{80,96},{96,112},{1,17},{17... | collective-permute-start | bytes 6152 | tf_op jit(solution)/shard_map/ppermute | solution.py:18
  319.8 1.3 slice.188
  321.1 0.7 slice_add_fusion
  322.6 5.5 %collective-permute-start.2 = (f32[256,1]{0,1:T(1,128)S(1)}, f32[256,1]{0,1:T(1,128)S(1)}, u32[]{:S(2)}, u32[]{:S(2)}) collective-permute-start(f32[256,1]{0,1:T(1,128)S(1)} %slice.193), channel_id=1, source_target_pairs={{0,16},{16,32},{32,48},{48,64},{64,80},{80,96},{96,112},{1,17},{17... | collective-permute-start | bytes 3080 | tf_op jit(solution)/shard_map/ppermute | solution.py:28
  328.1 1.3 collective-permute-start.3
  329.4 6.1 %collective-permute-done.3 = f32[256,1]{0,1:T(1,128)S(1)} collective-permute-done((f32[256,1]{0,1:T(1,128)S(1)}, f32[256,1]{0,1:T(1,128)S(1)}, u32[]{:S(2)}, u32[]{:S(2)}) %collective-permute-start.3) | collective-permute-done | bytes 1056 | tf_op jit(solution)/shard_map/ppermute | solution.py:29
  335.4 0.9 concatenate.28
  336.3 0.9 fusion.82
  337.3 1.2 copy.23
  338.5 1.3 collective-permute-start.4
  340.0 3.0 collective-permute-start.5
  343.1 1.0 copy.24
  344.2 1.0 copy.26
  345.2 2.2 fusion.59
  347.4 6.3 %collective-permute-start.6 = (f32[256,2]{0,1:T(2,128)S(1)}, f32[256,2]{0,1:T(2,128)S(1)}, u32[]{:S(2)}, u32[]{:S(2)}) collective-permute-start(f32[256,2]{0,1:T(2,128)S(1)} %get-tuple-element.138), channel_id=1, source_target_pairs={{0,16},{16,32},{32,48},{48,64},{64,80},{80,96},{96,112},{1,17},{17... | collective-permute-start | bytes 6152 | tf_op jit(solution)/shard_map/ppermute | solution.py:28
  353.7 1.3 collective-permute-start.7
  355.0 5.7 %collective-permute-done.7 = f32[256,2]{0,1:T(2,128)S(1)} collective-permute-done((f32[256,2]{0,1:T(2,128)S(1)}, f32[256,2]{0,1:T(2,128)S(1)}, u32[]{:S(2)}, u32[]{:S(2)}) %collective-permute-start.7) | collective-permute-done | bytes 2080 | tf_op jit(solution)/shard_map/ppermute | solution.py:29
  360.7 4.9 concatenate.33
  365.6 92.0 %all-gather.2.cloned.1.call-done = f32[4096,1028]{0,1:T(8,128)} async-done(((f32[256,1028]{0,1:T(8,128)}), f32[4096,1028]{0,1:T(8,128)}) %all-gather.2.cloned.1.call-update) | async-done | bytes 16842768 | tf_op jit(solution)/shard_map/all_gather | solution.py:211
  457.6 39.5 %multiply_reduce_fusion = f32[512]{0:T(512)S(1)} fusion(f32[4096,1028]{0,1:T(8,128)} %all-gather.2.cloned.1.call-done, s32[512]{0:T(512)S(1)} %convert_element_type.62, f32[512]{0:T(512)S(1)} %sub.233, s32[512]{0:T(512)S(1)} %convert_element_type.65, s32[1028]{0:T(1024)S(1)} %iota_add_fusion.1, f32[512]{0:T(512)S(1)} %sub.241), kind=kOutput, calls=%fused_computation.44 | convolution fusion | flops 25890402304 | bytes 16857104 | tf_op jit(solution)/shard_map/dot_general | solution.py:146
  497.1 0.7 all_to_all.12
  497.8 6.8 %all-to-all-start.1 = ((f32[8,64,1]{1,2,0:T(1,128)}), f32[8,64,1]{1,2,0:T(1,128)S(1)}, u32[]{:S(2)}, u32[]{:S(2)}) async-start(f32[8,64,1]{1,2,0:T(1,128)} %bitcast.23), calls=%async_computation.2 | async-start | bytes 8192 | tf_op jit(solution)/shard_map/all_to_all | solution.py:213
  504.6 1.3 copy.28
  505.9 6.4 %all-to-all-done.1 = f32[8,64,1]{1,2,0:T(1,128)S(1)} async-done(((f32[8,64,1]{1,2,0:T(1,128)}), f32[8,64,1]{1,2,0:T(1,128)S(1)}, u32[]{:S(2)}, u32[]{:S(2)}) %all-to-all-start.1) | async-done | bytes 2080 | tf_op jit(solution)/shard_map/all_to_all | solution.py:213
  512.8 0.7 reduce.33
  513.5 0.8 convolution_bitcast_fusion
  (74 shorter events, 5.4 us)
Async XLA Ops:
  7.2 153.4 %reduce-scatter.7.cloned.1.call-start = ((), (), s32[]{:S(2)}) async-start(), calls=%async_computation.6 | async-start | bytes 1114112
  100.8 1.4 copy-start.1
  100.8 60.6 %copy-start = (f32[2,128]{1,0:T(2,128)S(1)}, f32[2,128]{1,0:T(2,128)}, u32[]{:S(2)}) copy-start(f32[2,128]{1,0:T(2,128)} %param.11) | copy-start | bytes 3076
  100.8 61.2 %copy-start.2 = (f32[128]{0:T(128)S(1)}, f32[128]{0:T(128)}, u32[]{:S(2)}) copy-start(f32[128]{0:T(128)} %param.12) | copy-start | bytes 1540
  163.3 14.3 %all-to-all-start = ((f32[8,1,320]{2,1,0:T(1,128)}), f32[8,1,320]{2,1,0:T(1,128)S(1)}, u32[]{:S(2)}, u32[]{:S(2)}) async-start(f32[8,1,320]{2,1,0:T(1,128)} %reshape.310), calls=%async_computation | async-start | bytes 24576 | tf_op jit(solution)/shard_map/all_to_all | solution.py:193
  169.8 140.6 %reduce-scatter.5.cloned.1.call-start = ((), (), s32[]{:S(2)}) async-start(), calls=%async_computation.4 | async-start | bytes 17965056 | tf_op jit(solution)/shard_map/reduce_scatter | solution.py:196
  216.9 240.7 %all-gather.2.cloned.1.call-start = ((), (), s32[]{:S(2)}) async-start(), calls=%async_computation.5 | async-start | bytes 17965056 | tf_op jit(solution)/shard_map/all_gather | solution.py:211
  311.2 10.0 %collective-permute-start = (f32[256,1]{0,1:T(1,128)S(1)}, f32[256,1]{0,1:T(1,128)S(1)}, u32[]{:S(2)}, u32[]{:S(2)}) collective-permute-start(f32[256,1]{0,1:T(1,128)S(1)} %slice.190), channel_id=1, source_target_pairs={{16,0},{32,16},{48,32},{64,48},{80,64},{96,80},{112,96},{17,1},{33... | collective-permute-start | bytes 3080 | tf_op jit(solution)/shard_map/ppermute | solution.py:18
  313.8 8.1 %collective-permute-start.1 = (f32[256,2]{0,1:T(2,128)S(1)}, f32[256,2]{0,1:T(2,128)S(1)}, u32[]{:S(2)}, u32[]{:S(2)}) collective-permute-start(f32[256,2]{0,1:T(2,128)S(1)} %slice.192), channel_id=1, source_target_pairs={{0,16},{16,32},{32,48},{48,64},{64,80},{80,96},{96,112},{1,17},{17... | collective-permute-start | bytes 6152 | tf_op jit(solution)/shard_map/ppermute | solution.py:18
  322.6 6.8 %collective-permute-start.2 = (f32[256,1]{0,1:T(1,128)S(1)}, f32[256,1]{0,1:T(1,128)S(1)}, u32[]{:S(2)}, u32[]{:S(2)}) collective-permute-start(f32[256,1]{0,1:T(1,128)S(1)} %slice.193), channel_id=1, source_target_pairs={{0,16},{16,32},{32,48},{48,64},{64,80},{80,96},{96,112},{1,17},{17... | collective-permute-start | bytes 3080 | tf_op jit(solution)/shard_map/ppermute | solution.py:28
  328.1 7.4 %collective-permute-start.3 = (f32[256,1]{0,1:T(1,128)S(1)}, f32[256,1]{0,1:T(1,128)S(1)}, u32[]{:S(2)}, u32[]{:S(2)}) collective-permute-start(f32[256,1]{0,1:T(1,128)S(1)} %slice.194), channel_id=1, source_target_pairs={{16,0},{32,16},{48,32},{64,48},{80,64},{96,80},{112,96},{17,1},{33... | collective-permute-start | bytes 3080 | tf_op jit(solution)/shard_map/ppermute | solution.py:29
  338.5 4.6 collective-permute-start.4
  340.0 4.1 collective-permute-start.5
  347.4 7.6 %collective-permute-start.6 = (f32[256,2]{0,1:T(2,128)S(1)}, f32[256,2]{0,1:T(2,128)S(1)}, u32[]{:S(2)}, u32[]{:S(2)}) collective-permute-start(f32[256,2]{0,1:T(2,128)S(1)} %get-tuple-element.138), channel_id=1, source_target_pairs={{0,16},{16,32},{32,48},{48,64},{64,80},{80,96},{96,112},{1,17},{17... | collective-permute-start | bytes 6152 | tf_op jit(solution)/shard_map/ppermute | solution.py:28
  353.7 7.0 %collective-permute-start.7 = (f32[256,2]{0,1:T(2,128)S(1)}, f32[256,2]{0,1:T(2,128)S(1)}, u32[]{:S(2)}, u32[]{:S(2)}) collective-permute-start(f32[256,2]{0,1:T(2,128)S(1)} %get-tuple-element.137), channel_id=1, source_target_pairs={{16,0},{32,16},{48,32},{64,48},{80,64},{96,80},{112,96},{17,1},{33... | collective-permute-start | bytes 6152 | tf_op jit(solution)/shard_map/ppermute | solution.py:29
  497.8 14.5 %all-to-all-start.1 = ((f32[8,64,1]{1,2,0:T(1,128)}), f32[8,64,1]{1,2,0:T(1,128)S(1)}, u32[]{:S(2)}, u32[]{:S(2)}) async-start(f32[8,64,1]{1,2,0:T(1,128)} %bitcast.23), calls=%async_computation.2 | async-start | bytes 8192 | tf_op jit(solution)/shard_map/all_to_all | solution.py:213
Sparse Core Ops, SparseCore 0:
  102.3 58.1 reduce-scatter.6
  217.0 93.4 reduce-scatter.4
  365.7 91.8 all-gather.1
